TPU v7x, 256 devices: a whole 4x4x8 slice. The times are simulated.
256 devices in a mesh: dp: 8 (over z), seq: 4 (over x), mp: 8 (over y, core).
Axes of the slice: x: 4, y: 4, z: 8, core: 2. Of those that a mesh axis runs over, the one named last changes fastest.
Arguments:
- hidden: bfloat16 [8, 1024, 8192], P('dp', 'seq'), may hold values from -6 to 6
- norm_gain: float32 [8192], replicated, may hold values from 0.5 to 1.5
- w_query: bfloat16 [8192, 4096], P(('dp', 'seq'), 'mp'), may hold values from -0.0625 to 0.0625
- w_key: bfloat16 [1280, 4096], P(None, 'mp'), may hold values from -0.15625 to 0.15625
- w_value: bfloat16 [1280, 4096], P(None, 'mp'), may hold values from -0.15625 to 0.15625
- w_out: bfloat16 [4096, 8192], P('mp', ('dp', 'seq')), may hold values from -0.375 to 0.375
- gate_alpha: float32 [8192], P('mp'), may hold values from 0.3 to 1.5
- latents: bfloat16 [128, 64, 1280], P(('dp', 'seq')), may hold values from -410 to 410
- image_doc: int32 [128, 1], replicated, may hold values from 0 to 7; in each aligned block of 4 rows (0 to 3, 4 to 7, ...) at most 2 rows name the same one
- image_pos: int32 [128], replicated, may hold values from 0 to 1023
Outputs:
- cross_out: bfloat16 [8, 1024, 8192], P('dp', 'seq', 'mp')
Inputs may be any that keep to these rules, and one draw needn't show every extreme that they name: `image_doc`: in the rows of one device (aligned blocks of 4 images) at most 2 images belong to one document, and some block of every draw has exactly 2; every document has an image.
All inputs are finite; a program needn't handle non-finite values.
Results may differ from a plain program's by a relative error of at most 0.02.
The roundings to bfloat16 on the way count: a program that leaves them out, or rounds other values in their place, can miss the bound.
Values may be sent and summed in bfloat16 or wider, within the bound.
A program may use at most 128 MiB of HBM per device.

v0:
```python
import jax
import jax.numpy as jnp
from jax import lax
from jax.sharding import PartitionSpec as P

HEAD_DIM = 128
CAP = 2


epsilon = 1e-05


def slot_rank(doc_ids):
    item_count = doc_ids.shape[-1]
    same_doc = doc_ids[..., :, None] == doc_ids[..., None, :]
    before = jnp.arange(item_count)[:, None] < jnp.arange(item_count)[None, :]
    return jnp.sum((same_doc & before).astype(jnp.int32), axis=-2)


def make_routes(doc_ids, doc_count, capacity):
    ranked = slot_rank(doc_ids)
    target = (doc_ids[None, None, :] == jnp.arange(doc_count)[:, None, None]) & (
        ranked[None, None, :] == jnp.arange(capacity)[None, :, None]
    )
    return target.astype(jnp.bfloat16)


def on_device(
    hidden, norm_gain, w_query, w_key, w_value, w_out, gate_alpha, latents, image_doc, image_pos
):
    dp_count = lax.axis_size("dp")
    seq_count = lax.axis_size("seq")
    dp_index = lax.axis_index("dp")
    seq_index = lax.axis_index("seq")
    tok_rows = hidden.shape[1]
    img_count, lat_count, lat_width = latents.shape
    local_cols = w_query.shape[1]
    widened = hidden[0].astype(jnp.float32)
    normed = (
        widened
        * lax.rsqrt(jnp.mean(widened * widened, axis=-1, keepdims=True) + epsilon)
        * norm_gain
    ).astype(jnp.bfloat16)
    queries = jnp.dot(
        normed,
        lax.all_gather(w_query, ("dp", "seq"), axis=0, tiled=True),
        preferred_element_type=jnp.float32,
    ).astype(jnp.bfloat16)
    docs_grid = image_doc[:, 0].reshape(dp_count, seq_count, img_count)
    pos_grid = image_pos.reshape(dp_count, seq_count, img_count)
    own_docs = lax.dynamic_index_in_dim(
        lax.dynamic_index_in_dim(docs_grid, dp_index, 0, False), seq_index, 0, False
    )
    routing = make_routes(own_docs, dp_count, CAP).reshape(dp_count * CAP, img_count)
    outgoing = jnp.dot(
        routing,
        latents.reshape(img_count, lat_count * lat_width),
        preferred_element_type=jnp.float32,
    ).astype(jnp.bfloat16)
    arrived = lax.all_to_all(
        outgoing.reshape(dp_count, CAP * lat_count, lat_width),
        "dp",
        split_axis=0,
        concat_axis=0,
        tiled=True,
    )
    lat_rows = arrived.reshape(dp_count * CAP * lat_count, lat_width)
    keys_here = jnp.dot(lat_rows, w_key, preferred_element_type=jnp.float32).astype(jnp.bfloat16)
    values_here = jnp.dot(lat_rows, w_value, preferred_element_type=jnp.float32).astype(
        jnp.bfloat16
    )
    keys_all, values_all = (
        lax.all_gather(keys_here, "seq", axis=0, tiled=True),
        lax.all_gather(values_here, "seq", axis=0, tiled=True),
    )
    ranked = slot_rank(docs_grid)
    matches = (docs_grid[:, :, None, :] == dp_index) & (
        ranked[:, :, None, :] == jnp.arange(CAP)[None, None, :, None]
    )
    slot_pos = jnp.sum(jnp.where(matches, pos_grid[:, :, None, :], 0), axis=-1)
    slot_pos = jnp.where(jnp.any(matches, axis=-1), slot_pos, tok_rows * seq_count)
    key_pos = jnp.broadcast_to(
        jnp.transpose(slot_pos, (1, 0, 2))[..., None], (seq_count, dp_count, CAP, lat_count)
    ).reshape(-1)
    text_pos = seq_index * tok_rows + jnp.arange(tok_rows, dtype=jnp.int32)
    visible = key_pos[None, :] <= text_pos[:, None]
    present = jnp.any(visible, axis=1)
    heads_here = local_cols // HEAD_DIM
    query_heads = jnp.transpose(queries.reshape(tok_rows, heads_here, HEAD_DIM), (1, 0, 2))
    key_heads = jnp.transpose(keys_all.reshape(-1, heads_here, HEAD_DIM), (1, 0, 2))
    value_heads = jnp.transpose(values_all.reshape(-1, heads_here, HEAD_DIM), (1, 0, 2))

    def one_head(operands):
        query_one, key_one, value_one = operands
        scores = jnp.dot(query_one, key_one.T, preferred_element_type=jnp.float32) * HEAD_DIM ** (
            -0.5
        )
        scores = jnp.where(visible, scores, -1e30)
        row_max = jnp.max(scores, axis=-1, keepdims=True)
        weights = jnp.exp(scores - row_max)
        running = jnp.sum(weights, axis=-1, keepdims=True)
        mixed = (
            jnp.dot(weights.astype(jnp.bfloat16), value_one, preferred_element_type=jnp.float32)
            / running
        )
        return mixed.astype(jnp.bfloat16)

    head_out = lax.map(one_head, (query_heads, key_heads, value_heads))
    attended = jnp.transpose(head_out, (1, 0, 2)).reshape(tok_rows, local_cols)
    partial_value = jnp.dot(
        attended,
        lax.all_gather(w_out, ("dp", "seq"), axis=1, tiled=True),
        preferred_element_type=jnp.float32,
    )
    summed = lax.psum_scatter(
        partial_value.astype(jnp.bfloat16), "mp", scatter_dimension=1, tiled=True
    ).astype(jnp.float32)
    result = summed * jnp.tanh(gate_alpha) * present[:, None].astype(jnp.float32)
    return result.astype(jnp.bfloat16)[None]


def solution(mesh):
    placed = (
        P("dp", "seq", None),
        P(),
        P(("dp", "seq"), "mp"),
        P(None, "mp"),
        P(None, "mp"),
        P("mp", ("dp", "seq")),
        P("mp"),
        P(("dp", "seq"), None, None),
        P(),
        P(),
    )
    return jax.shard_map(
        on_device, mesh=mesh, in_specs=placed, out_specs=P("dp", "seq", "mp"), check_vma=False
    )
```

profile of v0, /device:TPU:6, one launch (start us, length us, event | category | flops | bytes accessed | tf_op | source)
XLA Modules:
  0.0 450.7 jit_solution(13939697680965986572)
XLA Ops:
  7.1 1.4 reduce.3
  9.0 1.6 copy.34
  10.6 2.3 convolution_convert_fusion
  12.9 3.6 reshape.137
  16.5 70.9 %all_to_all.5 = bf16[8,128,1280]{2,1,0:T(8,128)(2,1)S(1)} all-to-all(bf16[8,128,1280]{2,1,0:T(8,128)(2,1)} %reshape.137), channel_id=1, replica_groups=mesh['dp'=8,'seq'=4,'mp'=8] {'dp'}, dimensions={0} | all-to-all | bytes 5242880 | tf_op jit(solution)/shard_map/all_to_all | solution.py:60
  87.4 1.5 copy-done.1
  88.9 2.6 convolution_convert_fusion.3
  91.6 4.3 convolution_convert_fusion.2
  98.4 3.5 fusion.25
  101.9 35.1 %all-gather.7.cloned.1.call-done = bf16[4096,512]{1,0:T(8,128)(2,1)} async-done(((bf16[1024,512]{1,0:T(8,128)(2,1)}), bf16[4096,512]{1,0:T(8,128)(2,1)}) %all-gather.7.cloned.1.call-update) | async-done | bytes 4194320 | tf_op jit(solution)/shard_map/all_gather | solution.py:73
  137.0 4.9 %bitcast_bitcast_fusion.1 = bf16[4,4096,128]{2,1,0:T(8,128)(2,1)} fusion(bf16[4096,512]{1,0:T(8,128)(2,1)} %all-gather.7.cloned.1.call-done), kind=kLoop, calls=%fused_computation.29 | loop fusion | bytes 8388608 | tf_op jit(solution)/shard_map/transpose | solution.py:90
  141.9 48.2 %all-gather.9.cloned.1.call-done = bf16[4096,512]{1,0:T(8,128)(2,1)} async-done(((bf16[1024,512]{1,0:T(8,128)(2,1)}), bf16[4096,512]{1,0:T(8,128)(2,1)}) %all-gather.9.cloned.1.call-update) | async-done | bytes 4194320 | tf_op jit(solution)/shard_map/all_gather | solution.py:74
  190.1 4.8 %bitcast_bitcast_fusion = bf16[4,4096,128]{2,1,0:T(8,128)(2,1)} fusion(bf16[4096,512]{1,0:T(8,128)(2,1)} %all-gather.9.cloned.1.call-done), kind=kLoop, calls=%fused_computation.28 | loop fusion | bytes 8388608 | tf_op jit(solution)/shard_map/transpose | solution.py:91
  194.9 96.4 %all-gather.5.cloned.1.call-done = bf16[8192,512]{1,0:T(8,128)(2,1)} async-done(((bf16[256,512]{1,0:T(8,128)(2,1)}), bf16[8192,512]{1,0:T(8,128)(2,1)}) %all-gather.5.cloned.1.call-update) | async-done | bytes 8388624 | tf_op jit(solution)/shard_map/all_gather | solution.py:46
  291.3 7.0 %fusion.36 = bf16[32,4,8,128]{3,2,1,0:T(8,128)(2,1)S(1)} fusion(bf16[8192,512]{1,0:T(8,128)(2,1)} %all-gather.5.cloned.1.call-done, bf16[1,256,8192]{2,1,0:T(8,128)(2,1)} %param.12, f32[8192]{0:T(1024)S(1)} %copy-done.5, f32[256]{0:T(256)S(1)} %add_rsqrt_fusion), kind=kOutput, calls=%fused_computation.37 | convolution fusion | flops 2156003328 | bytes 12878848 | tf_op jit(solution)/shard_map/dot_general | solution.py:44
  298.4 20.4 %while.11 = (s32[]{:T(128)}, bf16[4,256,128]{1,2,0:T(8,128)(2,1)S(1)}, bf16[4,256,128]{2,1,0:T(8,128)(2,1)S(1)}, bf16[4,4096,128]{2,1,0:T(8,128)(2,1)}, bf16[4,4...) while((s32[]{:T(128)}, bf16[4,256,128]{1,2,0:T(8,128)(2,1)S(1)}, ...), condition=%wide.region_8.9_spmd.clone, body=%wide.region_5.8_spmd.clone.sunk | while | flops 545324544 | bytes 15096933 | solution.py:108
  298.4 2.1 fusion.61
  300.6 0.7 fusion.62
  301.3 2.1 fusion.63
  303.5 2.2 fusion.61
  305.7 0.7 fusion.62
  306.4 2.1 fusion.63
  308.7 2.1 fusion.61
  310.8 0.7 fusion.62
  311.5 2.1 fusion.63
  313.8 2.1 fusion.61
  315.9 0.7 fusion.62
  316.6 2.1 fusion.63
  318.9 76.0 %all-gather.11.cloned.1.call-done = bf16[512,8192]{1,0:T(8,128)(2,1)} async-done(((bf16[512,256]{1,0:T(8,128)(2,1)}), bf16[512,8192]{1,0:T(8,128)(2,1)}) %all-gather.11.cloned.1.call-update) | async-done | bytes 8388624 | tf_op jit(solution)/shard_map/all_gather | solution.py:112
  394.9 7.7 %convolution_convert_fusion.1 = bf16[256,8192]{1,0:T(8,128)(2,1)} fusion(bf16[256,512]{0,1:T(8,128)(2,1)S(1)} %bitcast.86, bf16[512,8192]{1,0:T(8,128)(2,1)} %all-gather.11.cloned.1.call-done), kind=kOutput, calls=%fused_computation.23 | convolution fusion | flops 2149580800 | bytes 12845056 | tf_op jit(solution)/shard_map/dot_general | solution.py:110
  403.4 38.8 %reduce-scatter.2.cloned.1.call-done = bf16[256,1024]{1,0:T(8,128)(2,1)} async-done(((bf16[256,8192]{1,0:T(8,128)(2,1)}), bf16[256,1024]{1,0:T(8,128)(2,1)}) %reduce-scatter.2.cloned.1.call-update) | async-done | bytes 524304 | tf_op jit(solution)/shard_map/reduce_scatter | solution.py:115
  442.2 2.0 fusion.39
  (57 shorter events, 4.8 us)
Async XLA Ops:
  6.5 82.4 %copy-start = (bf16[1280,512]{1,0:T(8,128)(2,1)S(1)}, bf16[1280,512]{1,0:T(8,128)(2,1)}, u32[]{:S(2)}) copy-start(bf16[1280,512]{1,0:T(8,128)(2,1)} %param.15) | copy-start | bytes 3932164
  6.5 130.5 %all-gather.7.cloned.1.call-start = ((), (), s32[]{:S(2)}) async-start(), calls=%async_computation.3 | async-start | bytes 5242880 | tf_op jit(solution)/shard_map/all_gather | solution.py:73
  87.4 1.5 copy-start.1
  88.9 2.7 copy-start.4
  91.5 6.2 %copy-start.3 = (s32[128]{0:T(128)S(1)}, s32[128]{0:T(128)}, u32[]{:S(2)}) copy-start(s32[128]{0:T(128)} %param.21) | copy-start | bytes 1540
  91.6 98.5 %all-gather.9.cloned.1.call-start = ((), (), s32[]{:S(2)}) async-start(), calls=%async_computation.4 | async-start | bytes 5242880 | tf_op jit(solution)/shard_map/all_gather | solution.py:74
  95.9 195.4 %all-gather.5.cloned.1.call-start = ((), (), s32[]{:S(2)}) async-start(), calls=%async_computation.2 | async-start | bytes 8650752 | tf_op jit(solution)/shard_map/all_gather | solution.py:46
  96.7 298.3 %all-gather.11.cloned.1.call-start = ((), (), s32[]{:S(2)}) async-start(), calls=%async_computation.5 | async-start | bytes 8650752 | tf_op jit(solution)/shard_map/all_gather | solution.py:112
  97.3 344.9 %reduce-scatter.2.cloned.1.call-start = ((), (), s32[]{:S(2)}) async-start(), calls=%async_computation.6 | async-start | bytes 4718592 | tf_op jit(solution)/shard_map/reduce_scatter | solution.py:115
  141.9 149.4 %copy-start.5 = (f32[8192]{0:T(1024)S(1)}, f32[8192]{0:T(1024)}, u32[]{:S(2)}) copy-start(f32[8192]{0:T(1024)} %param.13) | copy-start | bytes 98308
  402.7 0.7 copy-start.2
Sparse Core Ops, SparseCore 0:
  91.7 45.2 all-gather.6
  138.8 51.2 all-gather.8
  192.7 98.6 all-gather.4
  293.6 101.2 all-gather.10
  402.8 39.3 reduce-scatter.1
where the time goes:
time: 452 us; the launch traced here: 451 us
  waiting for transfers between devices  296 us (65%)
  blocking collectives  70.9 us (16%)
  matrix products  40.9 us (9%)
  local copies, waits for them, and re-layouts  18.5 us (4%)
  between operations  13.3 us (3%)
  other arithmetic  10.9 us (2%)
    all_gather x1, waiting for transfers between devices, on_device(): lax.all_gather(w_query, ('dp', 'seq'), axis=0, tiled=True)  96.4 us
    all_gather x1, waiting for transfers between devices, on_device(): lax.all_gather(w_out, ('dp', 'seq'), axis=1, tiled=True)  76 us
    all_to_all x1, blocking collectives, on_device(): lax.all_to_all(outgoing.reshape(dp_count, CAP * lat_count, lat_width), 'd...  70.9 us
    all_gather x1, waiting for transfers between devices, on_device(): lax.all_gather(values_here, 'seq', axis=0, tiled=True)  48.2 us
    reduce_scatter x1, waiting for transfers between devices, on_device(): lax.psum_scatter(partial_value.astype(jnp.bfloat16), 'mp', scatter_dimens...  38.8 us
    all_gather x1, waiting for transfers between devices, on_device(): lax.all_gather(keys_here, 'seq', axis=0, tiled=True)  35.1 us
  transfers between devices with their start and end apart: 5, of which 5 were waited for; matrix products, arithmetic and copies ran while one was open for 10% of the time, Pallas kernels for 0%

commit v1 on v0

v1 whole, which is shorter than its diff:
```python
import functools

import jax
import jax.numpy as jnp
from jax import lax
from jax.experimental import pallas as pl
from jax.experimental.pallas import tpu as pltpu
from jax.sharding import PartitionSpec as P

HEAD_DIM = 128
EPSILON = 1e-05
NZ, NX, NM, NY = 8, 4, 8, 4
LOG2E = 1.4426950408889634
MASKED = -1e30
FAR = 1 << 20
BF16, F32 = jnp.bfloat16, jnp.float32


def dot(a, b):
    return jnp.dot(a, b, preferred_element_type=F32)


def kernel(
    hidden, gain, w_query, w_key, w_value, w_out, gate, latents, doc_ref, pos_ref,
    out,
    hid_v, lat_v, wk_v, wv_v, lat_out, lat_all, norm_out, norm_all, wq_all, wo_all,
    kv_out, kv_all, key_pos, q_out, q_in, scores, att_all,
    pair_out, pair_own, pair_in, sum_out, sum_in, fin_out,
    send_sems, recv_sems, local_sems,
):
    z, x, m = lax.axis_index("dp"), lax.axis_index("seq"), lax.axis_index("mp")
    y, c = m // 2, lax.rem(m, 2)
    sibling = (z, x, m + 1 - 2 * c)

    def at_z(off):
        return (lax.rem(z + off + NZ, NZ), x, m)

    def at_x(off):
        return (z, lax.rem(x + off, NX), m)

    def at_y(off):
        return (z, x, lax.rem(m + 2 * off, NM))

    taken = [0]
    sent = []

    def remote(src, dst, device):
        slot = taken[0]
        taken[0] += 1
        return pltpu.make_async_remote_copy(
            src_ref=src, dst_ref=dst, send_sem=send_sems.at[slot], recv_sem=recv_sems.at[slot],
            device_id=device, device_id_type=pl.DeviceIdType.MESH,
        )

    def start(copy):
        copy.start()
        sent.append(copy)

    tok_part = pl.ds(pl.multiple_of(m * 32, 32), 32)
    lat_part = pl.ds(pl.multiple_of(lax.rem(m, 4) * 16, 16), 16)
    loads = [
        pltpu.make_async_copy(s, d, local_sems.at[i])
        for i, (s, d) in enumerate((
            (latents.at[:, lat_part, :], lat_v),
            (hidden.at[0, tok_part, :], hid_v),
            (w_key, wk_v),
            (w_value, wv_v),
            (w_query, wq_all.at[z]),
            (w_out, wo_all.at[z]),
        ))
    ]
    for load in loads:
        load.start()

    partners = [at_z(o) for o in range(1, NZ)] + [at_x(o) for o in range(1, NX)]
    partners += [at_y(o) for o in range(1, NY)] + [sibling]
    barrier = pltpu.get_barrier_semaphore()
    for partner in partners:
        pl.semaphore_signal(
            barrier, inc=1, device_id=partner, device_id_type=pl.DeviceIdType.MESH
        )
    pl.semaphore_wait(barrier, len(partners))

    def make_ring(own, buf):
        half = own.shape[0] // 2
        steps = []
        for s in range(4):
            up_from, down_from = lax.rem(z - s + NZ, NZ), lax.rem(z + s, NZ)
            up, down = buf.at[up_from], buf.at[down_from]
            if s == 3:
                up, down = buf.at[up_from, pl.ds(0, half)], buf.at[down_from, pl.ds(half, half)]
            steps.append((
                remote(own if s == 0 else up, up, at_z(1)),
                remote(own if s == 0 else down, down, at_z(-1)),
            ))
        return steps

    ring_q = make_ring(w_query, wq_all)
    ring_o = make_ring(w_out, wo_all)

    def ring_start(ring, s):
        if s > 0:
            ring_wait(ring, s - 1)
        for copy in ring[s]:
            start(copy)

    def ring_wait(ring, s):
        for copy in ring[s]:
            copy.wait_recv()

    base = (z * NX + x) * 4
    docs = [doc_ref[0, base + i] for i in range(4)]
    ranks = []
    for i in range(4):
        rank = jnp.int32(0)
        for before in range(i):
            rank = rank + jnp.where(docs[before] == docs[i], 1, 0)
        ranks.append(rank)
    slot_here = m // 4
    loads[0].wait()

    def route(doc, carry):
        total = None
        for i in range(4):
            chosen = (docs[i] == doc) & (ranks[i] == slot_here)
            term = lat_v[i].astype(F32) * jnp.where(chosen, 1.0, 0.0).astype(F32)
            total = term if total is None else total + term
        lat_out[doc] = total.astype(BF16)
        return carry

    lax.fori_loop(0, NZ, route, 0)
    lat_z = []
    for o in range(1, NZ):
        target = at_z(o)
        copy = remote(lat_out.at[target[0]], lat_all.at[m, z], target)
        start(copy)
        lat_z.append(copy)
    lat_all[m, z] = lat_out[z]
    ring_start(ring_q, 0)

    loads[1].wait()

    def square_sum(i, total):
        part = hid_v[:, pl.ds(pl.multiple_of(i * 1024, 1024), 1024)].astype(F32)
        return total + jnp.sum(part * part, axis=-1, keepdims=True)

    mean_square = lax.fori_loop(0, 8, square_sum, jnp.zeros((32, 1), F32)) / 8192.0
    inverse = lax.rsqrt(mean_square + EPSILON)

    def normalise(i, carry):
        cols = pl.ds(pl.multiple_of(i * 1024, 1024), 1024)
        rows = (hid_v[:, cols].astype(F32) * inverse * gain[:, cols]).astype(BF16)
        for owner in range(NX):
            norm_out[owner, :, pl.ds(pl.multiple_of(i * 256, 256), 256)] = rows[
                :, owner * 256 : owner * 256 + 256
            ]
        return carry

    lax.fori_loop(0, 8, normalise, 0)
    hid_x = []
    for o in (1, 3, 2):
        target = at_x(o)
        copy = remote(norm_out.at[target[1]], norm_all.at[x, m], target)
        start(copy)
        hid_x.append(copy)
    norm_all[x, m] = norm_out[x]

    lane_owner = lax.broadcasted_iota(jnp.int32, (1, 128), 1) // 16

    def positions(source_z, first):
        for source_x in range(NX):
            block = (source_z * NX + source_x) * 4
            slot_pos = [jnp.int32(FAR), jnp.int32(FAR)]
            seen = jnp.int32(0)
            for i in range(4):
                match = doc_ref[0, block + i] == z
                place = pos_ref[0, block + i]
                for r in range(2):
                    slot_pos[r] = jnp.where(match & (seen == r), place, slot_pos[r])
                seen = seen + jnp.where(match, 1, 0)
            for r in range(2):
                key_pos[source_x * 2 + r] = jnp.where(
                    lane_owner == source_z, slot_pos[r], key_pos[source_x * 2 + r]
                )
                first = jnp.minimum(first, slot_pos[r])
        return first

    key_pos[...] = jnp.full(key_pos.shape, FAR, jnp.int32)
    first_pos = lax.fori_loop(0, NZ, positions, jnp.int32(FAR))

    def make_gather(buf):
        along, across = {}, {}
        for o in (1, 3, 2):
            along[o] = remote(buf(m), buf(m), at_y(o))
        across[0] = remote(buf(m), buf(m), sibling)
        for o in (1, 3, 2):
            came = lax.rem(m - 2 * o + NM, NM)
            across[o] = remote(buf(came), buf(came), sibling)
        return along, across

    def gather_start(gather):
        along, across = gather
        for o in (1, 3, 2):
            start(along[o])
        start(across[0])

    def gather_pass(gather, o):
        along, across = gather
        along[o].wait_recv()
        start(across[o])

    lat_gather = make_gather(lambda who: lat_all.at[who])
    hid_gather = [make_gather(lambda who, k=k: norm_all.at[k, who]) for k in range(NX)]

    ring_start(ring_q, 1)
    for copy in lat_z:
        copy.wait_recv()
    gather_start(lat_gather)

    for copy in hid_x:
        copy.wait_recv()
    for k in range(NX):
        gather_start(hid_gather[k])

    kv_sends = []

    def keys_values(o):
        chip = lax.rem(y - o + NY, NY)
        rows = lat_all[pl.ds(chip * 2, 2)].reshape(256, 1280)
        for weight, at in ((wk_v, 0), (wv_v, HEAD_DIM)):
            made = dot(rows, weight[...]).astype(BF16)
            for head in range(NX):
                kv_out[head, chip, :, at : at + HEAD_DIM] = made[
                    :, head * HEAD_DIM : (head + 1) * HEAD_DIM
                ]
        for off in (1, 3, 2):
            target = at_x(off)
            copy = remote(kv_out.at[target[1], chip], kv_all.at[x, chip], target)
            start(copy)
            kv_sends.append(copy)
        kv_all[x, chip] = kv_out[x, chip]

    loads[2].wait()
    loads[3].wait()
    lat_gather[1][0].wait_recv()
    keys_values(0)
    ring_start(ring_q, 2)
    for o in (1, 3, 2):
        gather_pass(lat_gather, o)
        lat_gather[1][o].wait_recv()
        keys_values(o)
        if o == 3:
            ring_start(ring_q, 3)

    ring_wait(ring_q, 3)
    ring_start(ring_o, 0)
    loads[4].wait()
    q_sends = []
    for k in range(NX):
        for o in (1, 3, 2):
            gather_pass(hid_gather[k], o)
        for o in (0, 1, 3, 2):
            hid_gather[k][1][o].wait_recv()
        made = dot(norm_all[k].reshape(256, 2048), wq_all[...].reshape(2048, 512))
        for head in range(NX):
            q_out[k, head] = made[:, head * HEAD_DIM : (head + 1) * HEAD_DIM]
        copies = []
        for off in (1, 3, 2):
            target = at_x(off)
            copy = remote(q_out.at[k, target[1]], q_in.at[k, x], target)
            start(copy)
            copies.append(copy)
        q_sends.append(copies)
        if k < 3:
            ring_start(ring_o, k + 1)

    for copy in kv_sends:
        copy.wait_recv()

    head_lanes = pl.ds(pl.multiple_of(x * HEAD_DIM, HEAD_DIM), HEAD_DIM)
    att_sends = {}

    def attend(k):
        for copy in q_sends[k]:
            copy.wait_recv()
        query = q_out[k, x]
        for off in (1, 3, 2):
            query = query + q_in[k, lax.rem(x - off + NX, NX)]
        query = query.astype(BF16)
        text_pos = lax.broadcasted_iota(jnp.int32, (256, 128), 0) + k * 256

        def score(i, top):
            block = kv_all[i // 2, pl.ds(lax.rem(i, 2) * 2, 2)].reshape(512, 256)
            raw = lax.dot_general(
                query, block[:, :HEAD_DIM], (((1,), (1,)), ((), ())), preferred_element_type=F32
            )
            visible = key_pos[i] <= text_pos
            for g in range(4):
                part = jnp.where(visible, raw[:, g * 128 : (g + 1) * 128], MASKED)
                scores[i, :, g * 128 : (g + 1) * 128] = part
                top = jnp.maximum(top, part)
            return top

        top = lax.fori_loop(0, 8, score, jnp.full((256, 128), MASKED, F32))
        row_max = jnp.max(top, axis=-1, keepdims=True)

        def mix(i, carry):
            mixed, running = carry
            weights = jnp.exp2((scores[i] - row_max) * (HEAD_DIM ** (-0.5) * LOG2E))
            for g in range(4):
                running = running + weights[:, g * 128 : (g + 1) * 128]
            block = kv_all[i // 2, pl.ds(lax.rem(i, 2) * 2, 2)].reshape(512, 256)
            return mixed + dot(weights.astype(BF16), block[:, HEAD_DIM:]), running

        zero = jnp.zeros((256, 128), F32)
        mixed, running = lax.fori_loop(0, 8, mix, (zero, zero))
        att_all[k, :, head_lanes] = (
            mixed / jnp.sum(running, axis=-1, keepdims=True)
        ).astype(BF16)
        copies = []
        for off in (1, 3, 2):
            copy = remote(att_all.at[k, :, head_lanes], att_all.at[k, :, head_lanes], at_x(off))
            start(copy)
            copies.append(copy)
        att_sends[k] = copies

    pair_sends, sum_sends = {}, {}

    def project(k):
        for copy in att_sends[k]:
            copy.wait_recv()
        rows = att_all[k]

        def other(i, carry):
            pair_out[k, i] = dot(rows, wo_all[2 * i + 1 - c]).astype(BF16)
            return carry

        lax.fori_loop(0, NY, other, 0)
        pair = remote(pair_out.at[k], pair_in.at[k], sibling)
        start(pair)

        def mine(i, carry):
            pair_own[k, i] = dot(rows, wo_all[2 * i + c]).astype(BF16)
            return carry

        lax.fori_loop(0, NY, mine, 0)
        pair.wait_recv()
        copies = []
        for off in (1, 3, 2):
            to = lax.rem(y + off, NY)
            sum_out[k, to] = (
                pair_own[k, to].astype(F32) + pair_in[k, to].astype(F32)
            ).astype(BF16)
            copy = remote(sum_out.at[k, to], sum_in.at[k, y], at_y(off))
            start(copy)
            copies.append(copy)
        sum_sends[k] = copies

    out_cols = pl.ds(pl.multiple_of(x * 256, 256), 256)
    gate_here = jnp.tanh(gate[:, out_cols])
    fin_sends = []

    def finish(k):
        for copy in sum_sends[k]:
            copy.wait_recv()
        total = pair_own[k, y].astype(F32) + pair_in[k, y].astype(F32)
        for off in (1, 3, 2):
            total = total + sum_in[k, lax.rem(y - off + NY, NY)].astype(F32)
        present = lax.broadcasted_iota(jnp.int32, (256, 256), 0) + k * 256 >= first_pos
        result = total * gate_here * jnp.where(present, 1.0, 0.0)
        fin_out[k] = result.astype(BF16)
        copy = pltpu.make_async_remote_copy(
            src_ref=fin_out.at[k], dst_ref=out.at[0, :, out_cols],
            send_sem=send_sems.at[taken[0] + k], recv_sem=recv_sems.at[taken[0] + NX + x],
            device_id=(z, k, m), device_id_type=pl.DeviceIdType.MESH,
        )
        keep = pltpu.make_async_copy(fin_out.at[k], out.at[0, :, out_cols], local_sems.at[6])

        @pl.when(x == k)
        def _():
            keep.start()

        @pl.when(x != k)
        def _():
            copy.start()

        fin_sends.append((copy, keep))

    ring_wait(ring_o, 3)
    loads[5].wait()
    attend(0)
    attend(1)
    project(0)
    attend(2)
    project(1)
    attend(3)
    project(2)
    project(3)
    first_fin = taken[0]
    for k in range(NX):
        finish(k)

    for off in (1, 3, 2):
        source = lax.rem(x - off + NX, NX)
        cols = pl.ds(pl.multiple_of(source * 256, 256), 256)
        pltpu.make_async_remote_copy(
            src_ref=fin_out.at[0], dst_ref=out.at[0, :, cols],
            send_sem=send_sems.at[first_fin], recv_sem=recv_sems.at[first_fin + NX + source],
            device_id=at_x(off), device_id_type=pl.DeviceIdType.MESH,
        ).wait_recv()
    for k, (copy, keep) in enumerate(fin_sends):

        @pl.when(x == k)
        def _():
            keep.wait()

        @pl.when(x != k)
        def _():
            copy.wait_send()

    for copy in sent:
        copy.wait_send()


def on_device(
    hidden, norm_gain, w_query, w_key, w_value, w_out, gate_alpha, latents, image_doc, image_pos
):
    vmem = pl.BlockSpec(memory_space=pltpu.VMEM)
    smem = pl.BlockSpec(memory_space=pltpu.SMEM)
    anywhere = pl.BlockSpec(memory_space=pl.ANY)
    buffer = pltpu.VMEM
    return pl.pallas_call(
        kernel,
        out_shape=jax.ShapeDtypeStruct((1, 256, 1024), BF16),
        in_specs=[
            anywhere, vmem, anywhere, anywhere, anywhere, anywhere, vmem, anywhere, smem, smem,
        ],
        out_specs=anywhere,
        scratch_shapes=[
            buffer((32, 8192), BF16),
            buffer((4, 16, 1280), BF16),
            buffer((1280, 512), BF16),
            buffer((1280, 512), BF16),
            buffer((NZ, 16, 1280), BF16),
            buffer((NM, NZ, 16, 1280), BF16),
            buffer((NX, 32, 2048), BF16),
            buffer((NX, NM, 32, 2048), BF16),
            buffer((NZ, 256, 512), BF16),
            buffer((NZ, 512, 256), BF16),
            buffer((NX, NY, 256, 256), BF16),
            buffer((NX, NY, 256, 256), BF16),
            buffer((NX * 2, 1, 128), jnp.int32),
            buffer((NX, NX, 256, 128), F32),
            buffer((NX, NX, 256, 128), F32),
            buffer((8, 256, 512), F32),
            buffer((NX, 256, 512), BF16),
            buffer((NX, NY, 256, 256), BF16),
            buffer((NX, NY, 256, 256), BF16),
            buffer((NX, NY, 256, 256), BF16),
            buffer((NX, NY, 256, 256), BF16),
            buffer((NX, NY, 256, 256), BF16),
            buffer((NX, 256, 256), BF16),
            pltpu.SemaphoreType.DMA((160,)),
            pltpu.SemaphoreType.DMA((160,)),
            pltpu.SemaphoreType.DMA((8,)),
        ],
        compiler_params=pltpu.CompilerParams(
            collective_id=0, has_side_effects=True, vmem_limit_bytes=56 * 2**20
        ),
    )(
        hidden, norm_gain.reshape(1, -1), w_query, w_key, w_value, w_out,
        gate_alpha.reshape(1, -1), latents, image_doc.reshape(1, -1), image_pos.reshape(1, -1),
    )


def solution(mesh):
    placed = (
        P("dp", "seq", None),
        P(),
        P(("dp", "seq"), "mp"),
        P(None, "mp"),
        P(None, "mp"),
        P("mp", ("dp", "seq")),
        P("mp"),
        P(("dp", "seq"), None, None),
        P(),
        P(),
    )
    return jax.shard_map(
        on_device, mesh=mesh, in_specs=placed, out_specs=P("dp", "seq", "mp"), check_vma=False
    )
```

time: 452 us -> 131 us (0.29)
  waiting for transfers between devices: 296 us -> 0 us
  Pallas kernels: 0 us -> 129 us
  blocking collectives: 70.9 us -> 0 us
  matrix products: 40.9 us -> 0 us
  local copies, waits for them, and re-layouts: 18.5 us -> 1.87 us
  between operations: 13.3 us -> 0.01 us
  other arithmetic: 10.9 us -> 0 us
    all_gather x4 -> x0, waiting for transfers between devices: 256 us -> none  [the longest x1 96.4 us: on_device(): lax.all_gather(w_query, ('dp', 'seq'), axis=0, tiled=True)]
    pallas_call x0 -> x1, Pallas kernels: none -> 129 us  [on_device(): pl.pallas_call(kernel, out_shape=jax.ShapeDtypeStruct((1, 256, 1024), BF1...]
    all_to_all x1 -> x0, blocking collectives: 70.9 us -> none  [on_device(): lax.all_to_all(outgoing.reshape(dp_count, CAP * lat_count, lat_width), 'd...]
    dot_general x13 -> x0, matrix products: 40.9 us -> none  [the longest x4 8.5 us: one_head(): jnp.dot(query_one, key_one.T, preferred_element_type=jnp.float32)]
    reduce_scatter x1 -> x0, waiting for transfers between devices: 38.8 us -> none  [on_device(): lax.psum_scatter(partial_value.astype(jnp.bfloat16), 'mp', scatter_dimens...]
    transpose x2 -> x0, local copies, waits for them, and re-layouts: 9.71 us -> none  [the longest x1 4.88 us: on_device(): jnp.transpose(keys_all.reshape(-1, heads_here, HEAD_DIM), (1, 0, 2))]
    reduce_sum x8 -> x0, other arithmetic: 6.58 us -> none  [the longest x1 3.5 us: on_device(): jnp.mean(widened * widened, axis=-1, keepdims=True) + epsilon]
  transfers between devices with their start and end apart: 5 -> 0, of which waited for: 5 -> 0; matrix products, arithmetic and copies ran while one was open for 10% -> 0% of each run, Pallas kernels for 0% -> 0%
where the time goes in v1:
time: 131 us
  Pallas kernels  129 us (98%)
  local copies, waits for them, and re-layouts  1.87 us (1%)
    pallas_call x1, Pallas kernels, on_device(): pl.pallas_call(kernel, out_shape=jax.ShapeDtypeStruct((1, 256, 1024), BF1...  129 us

profile of v1, /device:TPU:6, one launch (start us, length us, event | category | flops | bytes accessed | tf_op | source)
XLA Modules:
  0.0 130.9 jit_solution(1003195906334415101)
XLA Ops:
  0.0 129.1 %shard_map.100 = bf16[1,256,1024]{2,1,0:T(8,128)(2,1)} custom-call(bf16[1,256,8192]{2,1,0:T(8,128)(2,1)} %hidden.1, f32[1,8192]{1,0:T(1,128)} %bitcast.4, bf16[256,512]{1,0:T(8,128)(2,1)} %w_query.1, bf16[1280,512]{1,0:T(8,128)(2,1)} %w_key.1, bf16[1280,512]{1,0:T(8,128)(2,1)} %w_value.1, bf16[512,256]{1,0:T(8,128)(2,1)} %w_out.1, f32[1,1024]{1,0:T(1,128)} %bitcast.5, ...), custom_call_target="tpu_custom_call" | custom-call | tf_op jit(solution)/shard_map/pallas_call | solution.py:432
  129.1 1.9 %copy.12 = bf16[1,256,1024]{2,1,0:T(8,128)(2,1)} copy(bf16[1,256,1024]{2,1,0:T(8,128)(2,1)} %shard_map.100) | data formatting | bytes 1048576

commit v2 on v1

--- a/solution.py
+++ b/solution.py
@@ -24,8 +24,8 @@
     hidden, gain, w_query, w_key, w_value, w_out, gate, latents, doc_ref, pos_ref,
     out,
     hid_v, lat_v, wk_v, wv_v, lat_out, lat_all, norm_out, norm_all, wq_all, wo_all,
-    kv_out, kv_all, key_pos, q_out, q_in, scores, att_all,
-    pair_out, pair_own, pair_in, sum_out, sum_in, fin_out,
+    kv_out, kv_all, key_pos, q_out, q_mid, q_in, scores, att_all,
+    pair_out, pair_own, pair_in, sum_out, sum_mid, sum_in, fin_out,
     send_sems, recv_sems, local_sems,
 ):
     z, x, m = lax.axis_index("dp"), lax.axis_index("seq"), lax.axis_index("mp")
@@ -44,9 +44,14 @@
     taken = [0]
     sent = []
 
-    def remote(src, dst, device):
-        slot = taken[0]
-        taken[0] += 1
+    def take(count):
+        first = taken[0]
+        taken[0] += count
+        return first
+
+    def remote(src, dst, device, slot=None):
+        if slot is None:
+            slot = take(1)
         return pltpu.make_async_remote_copy(
             src_ref=src, dst_ref=dst, send_sem=send_sems.at[slot], recv_sem=recv_sems.at[slot],
             device_id=device, device_id_type=pl.DeviceIdType.MESH,
@@ -55,6 +60,14 @@
     def start(copy):
         copy.start()
         sent.append(copy)
+
+    partners = [at_z(o) for o in range(1, NZ)] + [at_x(o) for o in range(1, NX)]
+    partners += [at_y(o) for o in range(1, NY)] + [sibling]
+    barrier = pltpu.get_barrier_semaphore()
+    for partner in partners:
+        pl.semaphore_signal(
+            barrier, inc=1, device_id=partner, device_id_type=pl.DeviceIdType.MESH
+        )
 
     tok_part = pl.ds(pl.multiple_of(m * 32, 32), 32)
     lat_part = pl.ds(pl.multiple_of(lax.rem(m, 4) * 16, 16), 16)
@@ -72,15 +85,6 @@
     for load in loads:
         load.start()
 
-    partners = [at_z(o) for o in range(1, NZ)] + [at_x(o) for o in range(1, NX)]
-    partners += [at_y(o) for o in range(1, NY)] + [sibling]
-    barrier = pltpu.get_barrier_semaphore()
-    for partner in partners:
-        pl.semaphore_signal(
-            barrier, inc=1, device_id=partner, device_id_type=pl.DeviceIdType.MESH
-        )
-    pl.semaphore_wait(barrier, len(partners))
-
     def make_ring(own, buf):
         half = own.shape[0] // 2
         steps = []
@@ -129,6 +133,7 @@
         return carry
 
     lax.fori_loop(0, NZ, route, 0)
+    pl.semaphore_wait(barrier, len(partners))
     lat_z = []
     for o in range(1, NZ):
         target = at_z(o)
@@ -136,7 +141,6 @@
         start(copy)
         lat_z.append(copy)
     lat_all[m, z] = lat_out[z]
-    ring_start(ring_q, 0)
 
     loads[1].wait()
 
@@ -157,13 +161,63 @@
         return carry
 
     lax.fori_loop(0, 8, normalise, 0)
-    hid_x = []
+    hid_x_first = take(NX)
     for o in (1, 3, 2):
         target = at_x(o)
-        copy = remote(norm_out.at[target[1]], norm_all.at[x, m], target)
-        start(copy)
-        hid_x.append(copy)
+        start(remote(norm_out.at[target[1]], norm_all.at[x, m], target, hid_x_first + o))
     norm_all[x, m] = norm_out[x]
+
+    def make_gather(block, halves, first):
+        came = {o: lax.rem(m - 2 * o + NM, NM) for o in range(NY)}
+        along = {o: remote(block(m), block(m), at_y(o), first + i) for i, o in enumerate((1, 3))}
+        onward = {
+            o: remote(halves(came[o])[i], halves(came[o])[i], at_y(o), first + 2 + i)
+            for i, o in enumerate((1, 3))
+        }
+        across = {
+            o: remote(block(came[o]), block(came[o]), sibling, first + 4 + o) for o in range(NY)
+        }
+        return along, onward, across
+
+    def gather_start(gather):
+        along, onward, across = gather
+        start(along[1])
+        start(along[3])
+        start(across[0])
+
+    def gather_pass(gather):
+        along, onward, across = gather
+        for o in (1, 3):
+            along[o].wait_recv()
+            start(onward[o])
+            start(across[o])
+
+    def gather_last(gather):
+        along, onward, across = gather
+        for o in (1, 3):
+            onward[o].wait_recv()
+        start(across[2])
+
+    lat_gather = make_gather(
+        lambda who: lat_all.at[who],
+        lambda who: (lat_all.at[who, pl.ds(0, 4)], lat_all.at[who, pl.ds(4, 4)]),
+        take(8),
+    )
+    hid_first = take(8 * NX)
+
+    def hid_gather(k):
+        return make_gather(
+            lambda who: norm_all.at[k, who],
+            lambda who: (norm_all.at[k, who, pl.ds(0, 16)], norm_all.at[k, who, pl.ds(16, 16)]),
+            hid_first + 8 * k,
+        )
+
+    def hid_start(k):
+        along, onward, across = hid_gather(k)
+        for copy in (along[1], along[3], across[0]):
+            copy.start()
+
+    hid_start(x)
 
     lane_owner = lax.broadcasted_iota(jnp.int32, (1, 128), 1) // 16
 
@@ -188,40 +242,10 @@
     key_pos[...] = jnp.full(key_pos.shape, FAR, jnp.int32)
     first_pos = lax.fori_loop(0, NZ, positions, jnp.int32(FAR))
 
-    def make_gather(buf):
-        along, across = {}, {}
-        for o in (1, 3, 2):
-            along[o] = remote(buf(m), buf(m), at_y(o))
-        across[0] = remote(buf(m), buf(m), sibling)
-        for o in (1, 3, 2):
-            came = lax.rem(m - 2 * o + NM, NM)
-            across[o] = remote(buf(came), buf(came), sibling)
-        return along, across
-
-    def gather_start(gather):
-        along, across = gather
-        for o in (1, 3, 2):
-            start(along[o])
-        start(across[0])
-
-    def gather_pass(gather, o):
-        along, across = gather
-        along[o].wait_recv()
-        start(across[o])
-
-    lat_gather = make_gather(lambda who: lat_all.at[who])
-    hid_gather = [make_gather(lambda who, k=k: norm_all.at[k, who]) for k in range(NX)]
-
-    ring_start(ring_q, 1)
     for copy in lat_z:
         copy.wait_recv()
     gather_start(lat_gather)
-
-    for copy in hid_x:
-        copy.wait_recv()
-    for k in range(NX):
-        gather_start(hid_gather[k])
-
+    ring_start(ring_q, 0)
     kv_sends = []
 
     def keys_values(o):
@@ -242,37 +266,77 @@
 
     loads[2].wait()
     loads[3].wait()
-    lat_gather[1][0].wait_recv()
+    lat_gather[2][0].wait_recv()
     keys_values(0)
+    ring_start(ring_q, 1)
+    gather_pass(lat_gather)
+    for k in range(NX):
+
+        @pl.when(x != k)
+        def _():
+            off = lax.rem(x - k + NX, NX)
+            remote(norm_out.at[k], norm_all.at[k, m], at_x(off), hid_x_first + off).wait_recv()
+            hid_start(k)
+
+    hid_gathers = [hid_gather(k) for k in range(NX)]
+    for gather in hid_gathers:
+        sent.extend((gather[0][1], gather[0][3], gather[2][0]))
+    for o in (1, 3):
+        lat_gather[2][o].wait_recv()
+        keys_values(o)
     ring_start(ring_q, 2)
-    for o in (1, 3, 2):
-        gather_pass(lat_gather, o)
-        lat_gather[1][o].wait_recv()
-        keys_values(o)
-        if o == 3:
-            ring_start(ring_q, 3)
+    gather_last(lat_gather)
+    gather_pass(hid_gathers[0])
+    lat_gather[2][2].wait_recv()
+    keys_values(2)
+    gather_pass(hid_gathers[1])
+    gather_last(hid_gathers[0])
+    ring_start(ring_q, 3)
+    gather_pass(hid_gathers[2])
+    gather_last(hid_gathers[1])
 
     ring_wait(ring_q, 3)
     ring_start(ring_o, 0)
     loads[4].wait()
-    q_sends = []
+    halves = {1: pl.ds(0, 128), 3: pl.ds(128, 128)}
+    far = lax.rem(x + 2, NX)
+    q_far, q_near = [], []
     for k in range(NX):
-        for o in (1, 3, 2):
-            gather_pass(hid_gather[k], o)
-        for o in (0, 1, 3, 2):
-            hid_gather[k][1][o].wait_recv()
+        q_far.append({
+            o: remote(q_out.at[k, far, halves[o]], q_mid.at[k, halves[o]], at_x(o))
+            for o in (1, 3)
+        })
+        q_near.append({
+            o: remote(q_out.at[k, at_x(o)[1]], q_in.at[k, i], at_x(o))
+            for i, o in enumerate((1, 3))
+        })
+
+    def send_near(k):
+        for o in (1, 3):
+            q_far[k][o].wait_recv()
+            to = at_x(o)[1]
+            q_out[k, to, halves[o]] = q_out[k, to, halves[o]] + q_mid[k, halves[o]]
+            start(q_near[k][o])
+
+    def ask(k):
+        for o in range(NY):
+            hid_gathers[k][2][o].wait_recv()
         made = dot(norm_all[k].reshape(256, 2048), wq_all[...].reshape(2048, 512))
         for head in range(NX):
             q_out[k, head] = made[:, head * HEAD_DIM : (head + 1) * HEAD_DIM]
-        copies = []
-        for off in (1, 3, 2):
-            target = at_x(off)
-            copy = remote(q_out.at[k, target[1]], q_in.at[k, x], target)
-            start(copy)
-            copies.append(copy)
-        q_sends.append(copies)
-        if k < 3:
-            ring_start(ring_o, k + 1)
+        for o in (1, 3):
+            start(q_far[k][o])
+
+    ask(0)
+    gather_pass(hid_gathers[3])
+    gather_last(hid_gathers[2])
+    ask(1)
+    send_near(0)
+    gather_last(hid_gathers[3])
+    ring_start(ring_o, 1)
+    ask(2)
+    send_near(1)
+    ask(3)
 
     for copy in kv_sends:
         copy.wait_recv()
@@ -281,12 +345,9 @@
     att_sends = {}
 
     def attend(k):
-        for copy in q_sends[k]:
-            copy.wait_recv()
-        query = q_out[k, x]
-        for off in (1, 3, 2):
-            query = query + q_in[k, lax.rem(x - off + NX, NX)]
-        query = query.astype(BF16)
+        for o in (1, 3):
+            q_near[k][o].wait_recv()
+        query = (q_out[k, x] + q_in[k, 0] + q_in[k, 1]).astype(BF16)
         text_pos = lax.broadcasted_iota(jnp.int32, (256, 128), 0) + k * 256
 
         def score(i, top):
@@ -301,7 +362,7 @@
                 top = jnp.maximum(top, part)
             return top
 
-        top = lax.fori_loop(0, 8, score, jnp.full((256, 128), MASKED, F32))
+        top = lax.fori_loop(0, 8, score, jnp.full((256, 128), MASKED, F32), unroll=True)
         row_max = jnp.max(top, axis=-1, keepdims=True)
 
         def mix(i, carry):
@@ -313,7 +374,7 @@
             return mixed + dot(weights.astype(BF16), block[:, HEAD_DIM:]), running
 
         zero = jnp.zeros((256, 128), F32)
-        mixed, running = lax.fori_loop(0, 8, mix, (zero, zero))
+        mixed, running = lax.fori_loop(0, 8, mix, (zero, zero), unroll=True)
         att_all[k, :, head_lanes] = (
             mixed / jnp.sum(running, axis=-1, keepdims=True)
         ).astype(BF16)
@@ -324,7 +385,11 @@
             copies.append(copy)
         att_sends[k] = copies
 
-    pair_sends, sum_sends = {}, {}
+    y_far = lax.rem(y + 2, NY)
+    pairs, sum_far, sum_near = {}, {}, {}
+
+    def chip_sum(k, to):
+        return pair_own[k, to].astype(F32) + pair_in[k, to].astype(F32)
 
     def project(k):
         for copy in att_sends[k]:
@@ -335,43 +400,55 @@
             pair_out[k, i] = dot(rows, wo_all[2 * i + 1 - c]).astype(BF16)
             return carry
 
-        lax.fori_loop(0, NY, other, 0)
-        pair = remote(pair_out.at[k], pair_in.at[k], sibling)
-        start(pair)
+        lax.fori_loop(0, NY, other, 0, unroll=True)
+        pairs[k] = remote(pair_out.at[k], pair_in.at[k], sibling)
+        start(pairs[k])
 
         def mine(i, carry):
             pair_own[k, i] = dot(rows, wo_all[2 * i + c]).astype(BF16)
             return carry
 
-        lax.fori_loop(0, NY, mine, 0)
-        pair.wait_recv()
-        copies = []
-        for off in (1, 3, 2):
-            to = lax.rem(y + off, NY)
-            sum_out[k, to] = (
-                pair_own[k, to].astype(F32) + pair_in[k, to].astype(F32)
-            ).astype(BF16)
-            copy = remote(sum_out.at[k, to], sum_in.at[k, y], at_y(off))
-            start(copy)
-            copies.append(copy)
-        sum_sends[k] = copies
+        lax.fori_loop(0, NY, mine, 0, unroll=True)
+
+    def send_sum(k):
+        pairs[k].wait_recv()
+        sum_out[k, y_far] = chip_sum(k, y_far).astype(BF16)
+        sum_far[k] = {}
+        for o in (1, 3):
+            sum_far[k][o] = remote(
+                sum_out.at[k, y_far, halves[o]], sum_mid.at[k, halves[o]], at_y(o)
+            )
+            start(sum_far[k][o])
+
+    def pass_sum(k):
+        sum_near[k] = {}
+        for i, o in enumerate((1, 3)):
+            to = lax.rem(y + o, NY)
+            total = chip_sum(k, to)
+            sum_far[k][o].wait_recv()
+            passed = sum_mid[k, halves[o]].astype(F32)
+            at = 0 if o == 1 else 128
+            sum_out[k, to, halves[o]] = (total[at : at + 128] + passed).astype(BF16)
+            rest = 128 - at
+            sum_out[k, to, halves[4 - o]] = total[rest : rest + 128].astype(BF16)
+            sum_near[k][o] = remote(sum_out.at[k, to], sum_in.at[k, i], at_y(o))
+            start(sum_near[k][o])
 
     out_cols = pl.ds(pl.multiple_of(x * 256, 256), 256)
     gate_here = jnp.tanh(gate[:, out_cols])
     fin_sends = []
+    first_fin = take(NX * 2)
 
     def finish(k):
-        for copy in sum_sends[k]:
-            copy.wait_recv()
-        total = pair_own[k, y].astype(F32) + pair_in[k, y].astype(F32)
-        for off in (1, 3, 2):
-            total = total + sum_in[k, lax.rem(y - off + NY, NY)].astype(F32)
+        for o in (1, 3):
+            sum_near[k][o].wait_recv()
+        total = chip_sum(k, y) + sum_in[k, 0].astype(F32) + sum_in[k, 1].astype(F32)
         present = lax.broadcasted_iota(jnp.int32, (256, 256), 0) + k * 256 >= first_pos
         result = total * gate_here * jnp.where(present, 1.0, 0.0)
         fin_out[k] = result.astype(BF16)
         copy = pltpu.make_async_remote_copy(
             src_ref=fin_out.at[k], dst_ref=out.at[0, :, out_cols],
-            send_sem=send_sems.at[taken[0] + k], recv_sem=recv_sems.at[taken[0] + NX + x],
+            send_sem=send_sems.at[first_fin + k], recv_sem=recv_sems.at[first_fin + NX + x],
             device_id=(z, k, m), device_id_type=pl.DeviceIdType.MESH,
         )
         keep = pltpu.make_async_copy(fin_out.at[k], out.at[0, :, out_cols], local_sems.at[6])
@@ -386,19 +463,32 @@
 
         fin_sends.append((copy, keep))
 
+    attend(0)
+    send_near(2)
+    ring_start(ring_o, 2)
+    attend(1)
+    send_near(3)
+    ring_start(ring_o, 3)
     ring_wait(ring_o, 3)
     loads[5].wait()
-    attend(0)
-    attend(1)
     project(0)
     attend(2)
+    send_sum(0)
     project(1)
     attend(3)
+    pass_sum(0)
+    send_sum(1)
     project(2)
+    pass_sum(1)
+    finish(0)
+    send_sum(2)
     project(3)
-    first_fin = taken[0]
-    for k in range(NX):
-        finish(k)
+    pass_sum(2)
+    finish(1)
+    send_sum(3)
+    finish(2)
+    pass_sum(3)
+    finish(3)
 
     for off in (1, 3, 2):
         source = lax.rem(x - off + NX, NX)
@@ -451,14 +541,16 @@
             buffer((NX, NY, 256, 256), BF16),
             buffer((NX * 2, 1, 128), jnp.int32),
             buffer((NX, NX, 256, 128), F32),
-            buffer((NX, NX, 256, 128), F32),
+            buffer((NX, 256, 128), F32),
+            buffer((NX, 2, 256, 128), F32),
             buffer((8, 256, 512), F32),
             buffer((NX, 256, 512), BF16),
             buffer((NX, NY, 256, 256), BF16),
             buffer((NX, NY, 256, 256), BF16),
             buffer((NX, NY, 256, 256), BF16),
             buffer((NX, NY, 256, 256), BF16),
-            buffer((NX, NY, 256, 256), BF16),
+            buffer((NX, 256, 256), BF16),
+            buffer((NX, 2, 256, 256), BF16),
             buffer((NX, 256, 256), BF16),
             pltpu.SemaphoreType.DMA((160,)),
             pltpu.SemaphoreType.DMA((160,)),

time: 131 us -> 116 us (0.89)
  Pallas kernels: 129 us -> 113 us
    pallas_call x1, Pallas kernels: 129 us -> 113 us  [on_device(): pl.pallas_call(kernel, out_shape=jax.ShapeDtypeStruct((1, 256, 1024), BF1...]
where the time goes in v2:
time: 116 us; the launch traced here: 115 us
  Pallas kernels  113 us (97%)
  local copies, waits for them, and re-layouts  1.87 us (2%)
    pallas_call x1, Pallas kernels, on_device(): pl.pallas_call(kernel, out_shape=jax.ShapeDtypeStruct((1, 256, 1024), BF1...  113 us

profile of v2, /device:TPU:6, one launch (start us, length us, event | category | flops | bytes accessed | tf_op | source)
XLA Modules:
  0.0 114.7 jit_solution(3451202133499748445)
XLA Ops:
  0.0 112.9 %shard_map.100 = bf16[1,256,1024]{2,1,0:T(8,128)(2,1)} custom-call(bf16[1,256,8192]{2,1,0:T(8,128)(2,1)} %hidden.1, f32[1,8192]{1,0:T(1,128)} %bitcast.4, bf16[256,512]{1,0:T(8,128)(2,1)} %w_query.1, bf16[1280,512]{1,0:T(8,128)(2,1)} %w_key.1, bf16[1280,512]{1,0:T(8,128)(2,1)} %w_value.1, bf16[512,256]{1,0:T(8,128)(2,1)} %w_out.1, f32[1,1024]{1,0:T(1,128)} %bitcast.5, ...), custom_call_target="tpu_custom_call" | custom-call | tf_op jit(solution)/shard_map/pallas_call | solution.py:522
  112.9 1.9 %copy.12 = bf16[1,256,1024]{2,1,0:T(8,128)(2,1)} copy(bf16[1,256,1024]{2,1,0:T(8,128)(2,1)} %shard_map.100) | data formatting | bytes 1048576

commit v3 on v2

--- a/solution.py
+++ b/solution.py
@@ -218,6 +218,7 @@
             copy.start()
 
     hid_start(x)
+    ring_start(ring_q, 0)
 
     lane_owner = lax.broadcasted_iota(jnp.int32, (1, 128), 1) // 16
 
@@ -245,7 +246,6 @@
     for copy in lat_z:
         copy.wait_recv()
     gather_start(lat_gather)
-    ring_start(ring_q, 0)
     kv_sends = []
 
     def keys_values(o):
@@ -292,11 +292,11 @@
     gather_pass(hid_gathers[1])
     gather_last(hid_gathers[0])
     ring_start(ring_q, 3)
+    ring_start(ring_o, 0)
     gather_pass(hid_gathers[2])
     gather_last(hid_gathers[1])
 
     ring_wait(ring_q, 3)
-    ring_start(ring_o, 0)
     loads[4].wait()
     halves = {1: pl.ds(0, 128), 3: pl.ds(128, 128)}
     far = lax.rem(x + 2, NX)
@@ -338,6 +338,7 @@
     send_near(1)
     ask(3)
 
+    ring_start(ring_o, 2)
     for copy in kv_sends:
         copy.wait_recv()
 
@@ -465,29 +466,28 @@
 
     attend(0)
     send_near(2)
-    ring_start(ring_o, 2)
+    ring_start(ring_o, 3)
+    send_near(3)
     attend(1)
-    send_near(3)
-    ring_start(ring_o, 3)
+    attend(2)
     ring_wait(ring_o, 3)
     loads[5].wait()
     project(0)
-    attend(2)
+    project(1)
     send_sum(0)
-    project(1)
     attend(3)
+    send_sum(1)
     pass_sum(0)
-    send_sum(1)
     project(2)
     pass_sum(1)
-    finish(0)
     send_sum(2)
     project(3)
+    finish(0)
+    send_sum(3)
     pass_sum(2)
     finish(1)
-    send_sum(3)
+    pass_sum(3)
     finish(2)
-    pass_sum(3)
     finish(3)
 
     for off in (1, 3, 2):

time: 116 us -> 107 us (0.922)
  Pallas kernels: 113 us -> 104 us
    pallas_call x1, Pallas kernels: 113 us -> 104 us  [on_device(): pl.pallas_call(kernel, out_shape=jax.ShapeDtypeStruct((1, 256, 1024), BF1...]
where the time goes in v3:
time: 107 us; the launch traced here: 106 us
  Pallas kernels  104 us (97%)
  local copies, waits for them, and re-layouts  1.87 us (2%)
    pallas_call x1, Pallas kernels, on_device(): pl.pallas_call(kernel, out_shape=jax.ShapeDtypeStruct((1, 256, 1024), BF1...  104 us

profile of v3, /device:TPU:6, one launch (start us, length us, event | category | flops | bytes accessed | tf_op | source)
XLA Modules:
  0.0 105.7 jit_solution(592719940691522255)
XLA Ops:
  0.0 103.8 %shard_map.100 = bf16[1,256,1024]{2,1,0:T(8,128)(2,1)} custom-call(bf16[1,256,8192]{2,1,0:T(8,128)(2,1)} %hidden.1, f32[1,8192]{1,0:T(1,128)} %bitcast.4, bf16[256,512]{1,0:T(8,128)(2,1)} %w_query.1, bf16[1280,512]{1,0:T(8,128)(2,1)} %w_key.1, bf16[1280,512]{1,0:T(8,128)(2,1)} %w_value.1, bf16[512,256]{1,0:T(8,128)(2,1)} %w_out.1, f32[1,1024]{1,0:T(1,128)} %bitcast.5, ...), custom_call_target="tpu_custom_call" | custom-call | tf_op jit(solution)/shard_map/pallas_call | solution.py:522
  103.8 1.9 %copy.12 = bf16[1,256,1024]{2,1,0:T(8,128)(2,1)} copy(bf16[1,256,1024]{2,1,0:T(8,128)(2,1)} %shard_map.100) | data formatting | bytes 1048576

commit v4 on v3

--- a/solution.py
+++ b/solution.py
@@ -285,6 +285,7 @@
         lat_gather[2][o].wait_recv()
         keys_values(o)
     ring_start(ring_q, 2)
+    ring_start(ring_o, 0)
     gather_last(lat_gather)
     gather_pass(hid_gathers[0])
     lat_gather[2][2].wait_recv()
@@ -292,7 +293,6 @@
     gather_pass(hid_gathers[1])
     gather_last(hid_gathers[0])
     ring_start(ring_q, 3)
-    ring_start(ring_o, 0)
     gather_pass(hid_gathers[2])
     gather_last(hid_gathers[1])
 
@@ -327,18 +327,18 @@
         for o in (1, 3):
             start(q_far[k][o])
 
+    ring_start(ring_o, 1)
     ask(0)
     gather_pass(hid_gathers[3])
     gather_last(hid_gathers[2])
     ask(1)
     send_near(0)
     gather_last(hid_gathers[3])
-    ring_start(ring_o, 1)
     ask(2)
+    ring_start(ring_o, 2)
     send_near(1)
     ask(3)
 
-    ring_start(ring_o, 2)
     for copy in kv_sends:
         copy.wait_recv()
 
@@ -469,15 +469,15 @@
     ring_start(ring_o, 3)
     send_near(3)
     attend(1)
-    attend(2)
     ring_wait(ring_o, 3)
     loads[5].wait()
     project(0)
+    attend(2)
+    send_sum(0)
     project(1)
-    send_sum(0)
     attend(3)
+    pass_sum(0)
     send_sum(1)
-    pass_sum(0)
     project(2)
     pass_sum(1)
     send_sum(2)

time: 107 us -> 109 us (1.019)
  Pallas kernels: 104 us -> 107 us
    pallas_call x1, Pallas kernels: 104 us -> 107 us  [on_device(): pl.pallas_call(kernel, out_shape=jax.ShapeDtypeStruct((1, 256, 1024), BF1...]
where the time goes in v4:
time: 109 us
  Pallas kernels  107 us (98%)
  local copies, waits for them, and re-layouts  1.87 us (2%)
    pallas_call x1, Pallas kernels, on_device(): pl.pallas_call(kernel, out_shape=jax.ShapeDtypeStruct((1, 256, 1024), BF1...  107 us

profile of v4, /device:TPU:6, one launch (start us, length us, event | category | flops | bytes accessed | tf_op | source)
XLA Modules:
  0.0 108.8 jit_solution(11354084344435552383)
XLA Ops:
  0.0 106.9 %shard_map.100 = bf16[1,256,1024]{2,1,0:T(8,128)(2,1)} custom-call(bf16[1,256,8192]{2,1,0:T(8,128)(2,1)} %hidden.1, f32[1,8192]{1,0:T(1,128)} %bitcast.4, bf16[256,512]{1,0:T(8,128)(2,1)} %w_query.1, bf16[1280,512]{1,0:T(8,128)(2,1)} %w_key.1, bf16[1280,512]{1,0:T(8,128)(2,1)} %w_value.1, bf16[512,256]{1,0:T(8,128)(2,1)} %w_out.1, f32[1,1024]{1,0:T(1,128)} %bitcast.5, ...), custom_call_target="tpu_custom_call" | custom-call | tf_op jit(solution)/shard_map/pallas_call | solution.py:522
  106.9 1.9 %copy.12 = bf16[1,256,1024]{2,1,0:T(8,128)(2,1)} copy(bf16[1,256,1024]{2,1,0:T(8,128)(2,1)} %shard_map.100) | data formatting | bytes 1048576
